TPU v7x, 32 devices: a whole 2x2x4 slice. The times are simulated.
32 devices in a mesh: groups: 2 (over y), lon: 4 (over z), lat: 4 (over x, core).
Axes of the slice: x: 2, y: 2, z: 4, core: 2. Of those that a mesh axis runs over, the one named last changes fastest.
Arguments:
- latent: bfloat16 [4, 96, 128, 320], P('groups', 'lat', 'lon'), parts along dimension 0, may hold values from -27 to 27
- band_index: int32 [96], P('lat'), may hold values from 0 to 7
- time_shift: float32 [4, 320], P('groups'), parts along dimension 0, may hold values from -4 to 4
- norm_gains: float32 [2, 320], replicated, may hold values from 0.1 to 1.9
- tap_scale: float32 [2, 8, 9, 320], replicated, may hold values from 0.5 to 2
- conv_one: bfloat16 [9, 320, 320], replicated, may hold values from -0.109375 to 0.109375
- conv_two: bfloat16 [9, 320, 320], replicated, may hold values from -0.109375 to 0.109375
Outputs:
- block_out: bfloat16 [4, 96, 128, 320], P('groups', 'lat', 'lon'), parts along dimension 0
There are 2 independent parts, one for each index of `groups`. A program takes and returns all parts, laid end to end along the dimension named above; an argument that names none is the same for every part. Nothing has to cross between parts.
All inputs are finite; a program needn't handle non-finite values.
Results may differ from a plain program's by a relative error of at most 0.0037.
Values may be sent and summed in bfloat16 or wider, within the bound.
A program may use at most 64 MiB of HBM per device.

v0:
```python
import jax
import jax.numpy as jnp
from jax import lax
from jax.sharding import PartitionSpec as P

NORM_GROUPS = 32
NB = 8


EPSILON = 1e-06


def padded_2(cells, sides, width, closed):
    for axis, dim in sides:
        count = lax.axis_size(axis)
        ends = count if closed else count - 1
        head = lax.slice_in_dim(cells, 0, width, axis=dim)
        tail = lax.slice_in_dim(cells, cells.shape[dim] - width, cells.shape[dim], axis=dim)
        cells = jnp.concatenate(
            [
                lax.ppermute(tail, axis, [(i, (i + 1) % count) for i in range(ends)]),
                cells,
                lax.ppermute(head, axis, [((i + 1) % count, i) for i in range(ends)]),
            ],
            axis=dim,
        )
    return cells


def norm_silu(field, gain):
    batch, rows_lat, cols_lon, chans = field.shape
    cells_count = (
        rows_lat * cols_lon * lax.axis_size("lon") * lax.axis_size("lat") * (chans // NORM_GROUPS)
    )
    grouped = field.reshape(batch, rows_lat, cols_lon, NORM_GROUPS, chans // NORM_GROUPS)
    summed = lax.psum(jnp.sum(grouped, axis=(1, 2, 4)), ("lon", "lat"))
    average = (summed / cells_count)[:, None, None, :, None]
    centred = grouped - average
    squares = lax.psum(jnp.sum(jnp.square(centred), axis=(1, 2, 4)), ("lon", "lat"))
    spread = (squares / cells_count)[:, None, None, :, None]
    normed = (centred * lax.rsqrt(spread + EPSILON)).reshape(batch, rows_lat, cols_lon, chans)
    return jax.nn.silu(normed * gain).astype(jnp.bfloat16)


def convolve(activation, kernel, row_scales):
    batch, rows_lat, cols_lon, chans = activation.shape
    widened = padded_2(activation, (("lon", 2),), 1, True)
    padded = padded_2(widened, (("lat", 1),), 1, False)
    total = jnp.zeros((batch, rows_lat, cols_lon, chans), jnp.float32)
    for tap_index in range(9):
        row_step, col_step = divmod(tap_index, 3)
        window = padded[
            :, row_step : row_step + rows_lat, col_step : col_step + cols_lon, :
        ].reshape(-1, chans)
        product = jnp.dot(window, kernel[tap_index], preferred_element_type=jnp.float32)
        total = (
            total
            + product.reshape(batch, rows_lat, cols_lon, chans)
            * row_scales[None, :, None, tap_index, :]
        )
    return total


def local(latent, band_index, time_shift, norm_gains, tap_scale, conv_one, conv_two):
    chans = latent.shape[3]
    one_hot = (band_index[:, None] == jnp.arange(NB, dtype=jnp.int32)[None, :]).astype(jnp.float32)
    table = tap_scale.reshape(2, NB, 9 * chans)
    row_scales = jnp.einsum("hn,knc->khc", one_hot, table, precision=lax.Precision.HIGHEST)
    row_scales = row_scales.reshape(2, band_index.shape[0], 9, chans)
    first = norm_silu(latent.astype(jnp.float32), norm_gains[0])
    middle = convolve(first, conv_one, row_scales[0]) + time_shift[:, None, None, :]
    second = norm_silu(middle, norm_gains[1])
    result = latent.astype(jnp.float32) + convolve(second, conv_two, row_scales[1])
    return result.astype(jnp.bfloat16)


def solution(mesh):
    return jax.shard_map(
        local,
        mesh=mesh,
        in_specs=(P("groups", "lat", "lon", None), P("lat"), P("groups", None), P(), P(), P(), P()),
        out_specs=P("groups", "lat", "lon", None),
        check_vma=False,
    )
```

profile of v0, /device:TPU:0, one launch (start us, length us, event | category | flops | bytes accessed | tf_op | source)
XLA Modules:
  0.0 187.0 jit_solution(17799416987220744411)
XLA Ops:
  0.0 1.6 convert_reduce_fusion
  2.6 34.9 %psum.28 = f32[2,32]{1,0:T(2,128)S(1)} all-reduce(f32[2,32]{1,0:T(2,128)S(1)} %reduce_sum.51), channel_id=1, replica_groups=mesh['groups'=2,'lon'=4,'lat'=4] {'lon','lat'}, use_global_device_ids=true, to_apply=%region_2.0 | all-reduce | flops 64 | bytes 512 | tf_op jit(solution)/shard_map/psum | solution.py:36
  37.7 1.6 fusion.2
  39.5 29.5 %psum.29 = f32[2,32]{1,0:T(2,128)S(1)} all-reduce(f32[2,32]{1,0:T(2,128)S(1)} %reduce_sum.54), channel_id=1, replica_groups=mesh['groups'=2,'lon'=4,'lat'=4] {'lon','lat'}, use_global_device_ids=true, to_apply=%region_5.6 | all-reduce | flops 64 | bytes 512 | tf_op jit(solution)/shard_map/psum | solution.py:39
  70.7 3.8 %collective-permute-start.1 = (bf16[2,24,1,320]{3,2,1,0:T(2,128)(2,1)}, bf16[2,24,1,320]{3,2,1,0:T(2,128)(2,1)}, u32[]{:S(2)}, u32[]{:S(2)}) collective-permute-start(bf16[2,24,1,320]{3,2,1,0:T(2,128)(2,1)} %get-tuple-element.18), channel_id=1, source_target_pairs={{4,0},{8,4},{12,8},{0,12},{5,1},{9,5},{13,9},{1,13},{6,2},{10,6},{... | collective-permute-start | bytes 92168 | tf_op jit(solution)/shard_map/ppermute | solution.py:23
  76.5 2.0 %fusion.55 = f32[2,24,32,320]{3,2,1,0:T(8,128)S(1)} fusion(bf16[2,24,32,320]{3,2,1,0:T(8,128)(2,1)S(1)} %fusion.9, bf16[9,320,320]{2,1,0:T(8,128)(2,1)} %param.12), kind=kOutput, calls=%fused_computation.70 | convolution fusion | flops 314572800 | bytes 3194880 | tf_op jit(solution)/shard_map/dot_general | solution.py:55
  82.5 1.3 collective-permute-start.2
  83.8 1.5 collective-permute-start.3
  85.2 1.7 fusion.31
  87.0 1.7 fusion.33
  88.8 2.6 %maximum_maximum_fusion = (bf16[2,25,34,320]{3,2,1,0:T(8,128)(2,1)S(1)}, bf16[2,25,34,320]{3,2,1,0:T(8,128)(2,1)S(1)}) fusion(bf16[2,24,1,320]{3,2,1,0:T(2,128)(2,1)} %collective-permute-done.1, bf16[2,24,32,320]{3,2,1,0:T(8,128)(2,1)S(1)} %fusion.9, bf16[2,24,1,320]{3,2,1,0:T(2,128)(2,1)} %collective-permute-done, ...), kind=kLoop, calls=%fused_computation.18 | loop fusion | flops 8704000 | bytes 3307520 | tf_op jit(solution)/shard_map/concatenate | solution.py:19
  91.4 0.9 fusion.35
  92.3 0.9 fusion.37
  93.1 0.9 fusion.39
  94.0 0.9 fusion.27
  94.9 0.9 fusion.29
  95.8 2.8 %fusion.91 = (f32[2,320]{1,0:T(2,128)S(1)}, f32[2,24,32,320]{3,2,1,0:T(8,128)S(1)}) fusion(f32[2,320]{1,0:T(2,128)S(1)} %copy-done.14, f32[24,320]{1,0:T(8,128)S(1)} %get-tuple-element.41, bf16[9,320,320]{2,1,0:T(8,128)(2,1)S(1)} %copy-done.2, bf16[2,25,34,320]{3,2,1,0:T(8,128)(2,1)S(1)} %get-tuple-element.12, f32[2,24,32,320]{3,2,1,0:T(8,128)S(1)} %fusion.27, ...), kind=kOutput, calls=%fused_computation.136 | convolution fusion | flops 323911040 | bytes 22603264 | tf_op jit(solution)/shard_map/dot_general | solution.py:55
  100.1 30.6 %psum.30 = f32[2,32]{1,0:T(2,128)S(1)} all-reduce(f32[2,32]{1,0:T(2,128)S(1)} %reduce_sum.72), channel_id=1, replica_groups=mesh['groups'=2,'lon'=4,'lat'=4] {'lon','lat'}, use_global_device_ids=true, to_apply=%region_8.9 | all-reduce | flops 64 | bytes 512 | tf_op jit(solution)/shard_map/psum | solution.py:36
  134.1 29.5 %psum.31 = f32[2,32]{1,0:T(2,128)S(1)} all-reduce(f32[2,32]{1,0:T(2,128)S(1)} %reduce_sum.75), channel_id=1, replica_groups=mesh['groups'=2,'lon'=4,'lat'=4] {'lon','lat'}, use_global_device_ids=true, to_apply=%region_11.12 | all-reduce | flops 64 | bytes 512 | tf_op jit(solution)/shard_map/psum | solution.py:39
  166.1 3.8 %collective-permute-start.5 = (bf16[2,24,1,320]{3,2,1,0:T(2,128)(2,1)S(1)}, bf16[2,24,1,320]{3,2,1,0:T(2,128)(2,1)S(1)}, u32[]{:S(2)}, u32[]{:S(2)}) collective-permute-start(bf16[2,24,1,320]{3,2,1,0:T(2,128)(2,1)S(1)} %get-tuple-element.16), channel_id=1, source_target_pairs={{4,0},{8,4},{12,8},{0,12},{5,1},{9,5},{13,9},{1,13},{6,2},{10,6},{... | collective-permute-start | bytes 92168 | tf_op jit(solution)/shard_map/ppermute | solution.py:23
  170.8 1.9 %collective-permute-done.4 = bf16[2,24,1,320]{3,2,1,0:T(2,128)(2,1)S(1)} collective-permute-done((bf16[2,24,1,320]{3,2,1,0:T(2,128)(2,1)S(1)}, bf16[2,24,1,320]{3,2,1,0:T(2,128)(2,1)S(1)}, u32[]{:S(2)}, u32[]{:S(2)}) %collective-permute-start.4) | collective-permute-done | bytes 30752 | tf_op jit(solution)/shard_map/ppermute | solution.py:21
  172.8 1.3 collective-permute-start.6
  174.1 1.3 collective-permute-start.7
  175.4 0.9 fusion.16
  176.2 0.9 fusion.18
  177.2 1.7 maximum_maximum_fusion.1
  178.9 0.9 fusion.20
  179.8 0.9 fusion.22
  180.7 0.9 fusion.24
  181.5 0.9 fusion.12
  182.5 0.9 fusion.14
  183.5 3.6 %fusion.10 = bf16[2,24,32,320]{3,2,1,0:T(8,128)(2,1)} fusion(bf16[2,24,32,320]{3,2,1,0:T(8,128)(2,1)S(1)} %copy-done, f32[2,24,32,320]{3,2,1,0:T(8,128)S(1)} %fusion.12, f32[2,24,32,320]{3,2,1,0:T(8,128)S(1)} %fusion.14, f32[2,24,32,320]{3,2,1,0:T(8,128)S(1)} %fusion.16, f32[2,24,32,320]{3,2,1,0:T(8,128)S(1)} %fusion.45, ...), kind=kOutput, calls=%fused_computation.14 | convolution fusion | flops 324403200 | bytes 22794240 | tf_op jit(solution)/shard_map/dot_general | solution.py:55
  (88 shorter events, 17.4 us)
Async XLA Ops:
  0.0 69.2 %copy-start = (bf16[2,24,32,320]{3,2,1,0:T(8,128)(2,1)S(1)}, bf16[2,24,32,320]{3,2,1,0:T(8,128)(2,1)}, u32[]{:S(2)}) copy-start(bf16[2,24,32,320]{3,2,1,0:T(8,128)(2,1)} %param.7) | copy-start | bytes 2949124
  1.6 73.0 %copy-start.12 = (f32[2,8,9,320]{3,1,2,0:T(8,128)S(1)}, f32[2,8,9,320]{3,1,2,0:T(8,128)}, u32[]{:S(2)}) copy-start(f32[2,8,9,320]{3,1,2,0:T(8,128)} %param.11) | copy-start | bytes 552964
  37.7 37.1 %copy-start.15 = (s32[24]{0:T(128)S(1)}, s32[24]{0:T(128)}, u32[]{:S(2)}) copy-start(s32[24]{0:T(128)} %param.8) | copy-start | bytes 292
  70.7 11.0 %collective-permute-start = (bf16[2,24,1,320]{3,2,1,0:T(2,128)(2,1)}, bf16[2,24,1,320]{3,2,1,0:T(2,128)(2,1)}, u32[]{:S(2)}, u32[]{:S(2)}) collective-permute-start(bf16[2,24,1,320]{3,2,1,0:T(2,128)(2,1)} %get-tuple-element.17), channel_id=1, source_target_pairs={{0,4},{4,8},{8,12},{12,0},{1,5},{5,9},{9,13},{13,1},{2,6},{6,10},{... | collective-permute-start | bytes 92168 | tf_op jit(solution)/shard_map/ppermute | solution.py:21
  70.7 11.0 %collective-permute-start.1 = (bf16[2,24,1,320]{3,2,1,0:T(2,128)(2,1)}, bf16[2,24,1,320]{3,2,1,0:T(2,128)(2,1)}, u32[]{:S(2)}, u32[]{:S(2)}) collective-permute-start(bf16[2,24,1,320]{3,2,1,0:T(2,128)(2,1)} %get-tuple-element.18), channel_id=1, source_target_pairs={{4,0},{8,4},{12,8},{0,12},{5,1},{9,5},{13,9},{1,13},{6,2},{10,6},{... | collective-permute-start | bytes 92168 | tf_op jit(solution)/shard_map/ppermute | solution.py:23
  76.3 2.2 %copy-start.13 = (f32[24,1,320]{2,1,0:T(1,128)S(1)}, f32[24,1,320]{2,1,0:T(1,128)}, u32[]{:S(2)}) copy-start(f32[24,1,320]{2,1,0:T(1,128)} %get-tuple-element.21) | copy-start | bytes 92164
  76.5 8.7 %copy-start.2 = (bf16[9,320,320]{2,1,0:T(8,128)(2,1)S(1)}, bf16[9,320,320]{2,1,0:T(8,128)(2,1)}, u32[]{:S(2)}) copy-start(bf16[9,320,320]{2,1,0:T(8,128)(2,1)} %param.12) | copy-start | bytes 5529604
  82.5 6.3 %collective-permute-start.2 = (bf16[2,1,34,320]{3,2,1,0:T(8,128)(2,1)S(1)}, bf16[2,1,34,320]{3,2,1,0:T(8,128)(2,1)S(1)}, u32[]{:S(2)}, u32[]{:S(2)}) collective-permute-start(bf16[2,1,34,320]{3,2,1,0:T(8,128)(2,1)S(1)} %get-tuple-element.13), channel_id=1, source_target_pairs={{0,1},{1,2},{2,3},{4,5},{5,6},{6,7},{8,9},{9,10},{10,11},{12,13},{... | collective-permute-start | bytes 130568 | tf_op jit(solution)/shard_map/ppermute | solution.py:21
  83.8 5.0 %collective-permute-start.3 = (bf16[2,1,34,320]{3,2,1,0:T(8,128)(2,1)S(1)}, bf16[2,1,34,320]{3,2,1,0:T(8,128)(2,1)S(1)}, u32[]{:S(2)}, u32[]{:S(2)}) collective-permute-start(bf16[2,1,34,320]{3,2,1,0:T(8,128)(2,1)S(1)} %get-tuple-element.14), channel_id=1, source_target_pairs={{1,0},{2,1},{3,2},{5,4},{6,5},{7,6},{9,8},{10,9},{11,10},{13,12},{... | collective-permute-start | bytes 130568 | tf_op jit(solution)/shard_map/ppermute | solution.py:23
  94.9 0.9 copy-start.14
  165.2 4.7 %copy-start.1 = (bf16[9,320,320]{2,1,0:T(8,128)(2,1)S(1)}, bf16[9,320,320]{2,1,0:T(8,128)(2,1)}, u32[]{:S(2)}) copy-start(bf16[9,320,320]{2,1,0:T(8,128)(2,1)} %param.13) | copy-start | bytes 5529604
  166.0 6.7 %collective-permute-start.4 = (bf16[2,24,1,320]{3,2,1,0:T(2,128)(2,1)S(1)}, bf16[2,24,1,320]{3,2,1,0:T(2,128)(2,1)S(1)}, u32[]{:S(2)}, u32[]{:S(2)}) collective-permute-start(bf16[2,24,1,320]{3,2,1,0:T(2,128)(2,1)S(1)} %get-tuple-element.15), channel_id=1, source_target_pairs={{0,4},{4,8},{8,12},{12,0},{1,5},{5,9},{9,13},{13,1},{2,6},{6,10},{... | collective-permute-start | bytes 92168 | tf_op jit(solution)/shard_map/ppermute | solution.py:21
  166.1 6.6 %collective-permute-start.5 = (bf16[2,24,1,320]{3,2,1,0:T(2,128)(2,1)S(1)}, bf16[2,24,1,320]{3,2,1,0:T(2,128)(2,1)S(1)}, u32[]{:S(2)}, u32[]{:S(2)}) collective-permute-start(bf16[2,24,1,320]{3,2,1,0:T(2,128)(2,1)S(1)} %get-tuple-element.16), channel_id=1, source_target_pairs={{4,0},{8,4},{12,8},{0,12},{5,1},{9,5},{13,9},{1,13},{6,2},{10,6},{... | collective-permute-start | bytes 92168 | tf_op jit(solution)/shard_map/ppermute | solution.py:23
  172.8 4.4 %collective-permute-start.6 = (bf16[2,1,34,320]{3,2,1,0:T(8,128)(2,1)S(1)}, bf16[2,1,34,320]{3,2,1,0:T(8,128)(2,1)S(1)}, u32[]{:S(2)}, u32[]{:S(2)}) collective-permute-start(bf16[2,1,34,320]{3,2,1,0:T(8,128)(2,1)S(1)} %get-tuple-element.9), channel_id=1, source_target_pairs={{0,1},{1,2},{2,3},{4,5},{5,6},{6,7},{8,9},{9,10},{10,11},{12,13},{... | collective-permute-start | bytes 130568 | tf_op jit(solution)/shard_map/ppermute | solution.py:21
  174.1 3.1 %collective-permute-start.7 = (bf16[2,1,34,320]{3,2,1,0:T(8,128)(2,1)S(1)}, bf16[2,1,34,320]{3,2,1,0:T(8,128)(2,1)S(1)}, u32[]{:S(2)}, u32[]{:S(2)}) collective-permute-start(bf16[2,1,34,320]{3,2,1,0:T(8,128)(2,1)S(1)} %get-tuple-element.10), channel_id=1, source_target_pairs={{1,0},{2,1},{3,2},{5,4},{6,5},{7,6},{9,8},{10,9},{11,10},{13,12},{... | collective-permute-start | bytes 130568 | tf_op jit(solution)/shard_map/ppermute | solution.py:23
  182.4 1.0 copy-start.3
  182.4 1.0 copy-start.4
  182.4 1.0 copy-start.5
  182.4 1.0 copy-start.6
  182.4 1.0 copy-start.7
  182.5 1.0 copy-start.8
  182.5 1.0 copy-start.9
  182.5 1.0 copy-start.10
  182.5 1.0 copy-start.11
where the time goes:
time: 189 us; the launch traced here: 187 us
  blocking collectives  124 us (66%)
  matrix products  23.4 us (12%)
  starting transfers between devices  13 us (7%)
  other arithmetic  12 us (6%)
  local copies, waits for them, and re-layouts  11.5 us (6%)
  waiting for transfers between devices  2.03 us (1%)
    psum x2, blocking collectives, norm_silu(): summed = lax.psum(jnp.sum(grouped, axis=(1, 2, 4)), ('lon', 'lat'))  65.5 us
    psum x2, blocking collectives, norm_silu(): lax.psum(jnp.sum(jnp.square(centred), axis=(1, 2, 4)), ('lon', 'lat'))  59 us
    dot_general x18, matrix products, convolve(): jnp.dot(window, kernel[tap_index], preferred_element_type=jnp.float32)  23 us
    ppermute x4, starting transfers between devices, padded_2(): lax.ppermute(head, axis, [((i + 1) % count, i) for i in range(ends)])  10.4 us
    concatenate x2, other arithmetic, padded_2(): jnp.concatenate([lax.ppermute(tail, axis, [(i, (i + 1) % count) for i in...  4.32 us
  transfers between devices with their start and end apart: 8, of which 2 were waited for; matrix products, arithmetic and copies ran while one was open for 7% of the time, Pallas kernels for 0%

commit v1 on v0

v1 whole, which is shorter than its diff:
```python
import functools

import jax
import jax.numpy as jnp
from jax import lax
from jax.experimental import pallas as pl
from jax.experimental.pallas import tpu as pltpu
from jax.sharding import PartitionSpec as P

NORM_GROUPS = 32
EPSILON = 1e-06
MESH = pl.DeviceIdType.MESH
F32 = jnp.float32
BF16 = jnp.bfloat16
WAYS = ((-1, 0), (1, 0), (0, -1), (0, 1), (-1, -1), (-1, 1), (1, -1), (1, 1))


def kernel(
    n_lon,
    n_lat,
    latent,
    band,
    time_shift,
    gains,
    tap_scale,
    conv_one,
    conv_two,
    out,
    field,
    act,
    weights,
    scales,
    row_halo,
    col_halo,
    corner_halo,
    col_send,
    corner_send,
    edge_act,
    stat_send,
    stat_recv,
    group_sum,
    weight_sem,
    halo_send_sem,
    halo_recv_sem,
    stat_send_sem,
    stat_recv_sem,
):
    batch, rows, cols, chans = latent.shape
    n = n_lon * n_lat
    per_group = chans // NORM_GROUPS
    local_count = float(rows * cols * per_group)
    whole_count = local_count * n
    lon = lax.axis_index("lon")
    lat = lax.axis_index("lat")
    me = lon * n_lat + lat

    def peer_id(step):
        peer = lax.rem(me + step, n)
        return {"lon": peer // n_lat, "lat": lax.rem(peer, n_lat)}

    barrier = pltpu.get_barrier_semaphore()

    @pl.loop(1, n)
    def _(step):
        pl.semaphore_signal(barrier, inc=1, device_id=peer_id(step), device_id_type=MESH)

    weight_copies = [
        pltpu.make_async_copy(src, weights.at[k], weight_sem.at[k])
        for k, src in enumerate((conv_one, conv_two))
    ]
    for copy in weight_copies:
        copy.start()

    def halo_copy(phase, b, way):
        d_lat, d_lon = WAYS[way]
        if d_lon == 0:
            top = d_lat < 0
            src = field.at[b, 0 if top else rows - 1]
            dst = row_halo.at[phase, b, 1 if top else 0]
        elif d_lat == 0:
            left = d_lon < 0
            src = col_send.at[phase, b, 0 if left else 1]
            dst = col_halo.at[phase, b, 1 if left else 0]
        else:
            mine = (0 if d_lat < 0 else 2) + (0 if d_lon < 0 else 1)
            src = corner_send.at[phase, b, mine]
            dst = corner_halo.at[phase, b, 3 - mine]
        return pltpu.make_async_remote_copy(
            src_ref=src,
            dst_ref=dst,
            send_sem=halo_send_sem.at[phase, b, way],
            recv_sem=halo_recv_sem.at[phase, b, way],
            device_id={
                "lon": lax.rem(lon + (d_lon + n_lon), n_lon),
                "lat": lat + d_lat,
            },
            device_id_type=MESH,
        )

    def when_lat(d_lat, body):
        if d_lat == 0:
            body()
        elif d_lat < 0:
            pl.when(lat > 0)(body)
        else:
            pl.when(lat < n_lat - 1)(body)

    def start_halos(phase, b):
        for side, col in ((0, 0), (1, cols - 1)):

            @pl.loop(0, rows)
            def _(r):
                col_send[phase, b, side, pl.ds(r, 1), :] = field[b, r, col : col + 1, :]

        for mine, (r, c) in enumerate(
            ((0, 0), (0, cols - 1), (rows - 1, 0), (rows - 1, cols - 1))
        ):
            corner_send[phase, b, mine] = field[b, r, c : c + 1, :]
        for way, (d_lat, _) in enumerate(WAYS):
            when_lat(d_lat, lambda way=way: halo_copy(phase, b, way).start())

    def wait_halos(phase, b):
        for way, (d_lat, _) in enumerate(WAYS):
            when_lat(d_lat, lambda way=way: halo_copy(phase, b, way).wait_send())
            when_lat(-d_lat, lambda way=way: halo_copy(phase, b, way).wait_recv())

    def over_group(per_chan):
        high = per_chan.astype(BF16).astype(F32)
        rest = per_chan - high
        middle = rest.astype(BF16).astype(F32)
        low = rest - middle
        line = lax.broadcasted_iota(jnp.int32, (16, chans), 0)
        parts = jnp.where(
            line == 0,
            high,
            jnp.where(line == 1, middle, jnp.where(line == 2, low, 0.0)),
        )
        summed = jnp.dot(parts.astype(BF16), group_sum[...], preferred_element_type=F32)
        return jnp.sum(summed, axis=0, keepdims=True)

    def fold(x):
        return jnp.sum(x.reshape(cols // 8, 8, chans), axis=0)

    def local_sum(b):
        def body(r, total):
            return total + fold(field[b, r])

        return lax.fori_loop(0, rows, body, jnp.zeros((8, chans), F32), unroll=4)

    def stat_copy(phase, b, step, span):
        return pltpu.make_async_remote_copy(
            src_ref=stat_send.at[phase, b] if span == 1 else stat_recv.at[phase, b, pl.ds(1, span)],
            dst_ref=stat_recv.at[phase, b, step]
            if span == 1
            else stat_recv.at[phase, b, pl.ds(1, span)],
            send_sem=stat_send_sem.at[phase, b],
            recv_sem=stat_recv_sem.at[phase, b],
            device_id=peer_id(step),
            device_id_type=MESH,
        )

    def local_stats(phase, b, total):
        summed = over_group(jnp.sum(total, axis=0, keepdims=True))
        average = summed * (1.0 / local_count)

        def body(r, squares):
            centred = field[b, r] - average
            return squares + fold(centred * centred)

        squares = lax.fori_loop(0, rows, body, jnp.zeros((8, chans), F32), unroll=4)
        squares = jnp.sum(squares, axis=0, keepdims=True)
        stat_send[phase, b, 0:1] = summed
        stat_send[phase, b, 1:2] = squares
        stat_recv[phase, b, 0, 0:1] = summed
        stat_recv[phase, b, 0, 1:2] = squares

    def start_stats(phase, b):
        @pl.loop(1, n)
        def _(step):
            stat_copy(phase, b, step, 1).start()

    def finish_stats(phase, b):
        stat_copy(phase, b, 1, n - 1).wait_recv()
        sums = stat_recv[phase, b, :, 0:1, :]
        squares = jnp.sum(stat_recv[phase, b, :, 1:2, :], axis=0)
        average = jnp.sum(sums, axis=0) * (1.0 / whole_count)
        apart = sums * (1.0 / local_count) - average[None]
        between = jnp.sum(apart * apart, axis=0) * local_count
        spread = (over_group(squares) + between) * (1.0 / whole_count)
        return average, lax.rsqrt(spread + EPSILON) * gains[phase : phase + 1, :] * 0.5

    def activate(phase, b, average, slope):
        def norm_silu(x):
            half = (x - average) * slope
            return half + half * jnp.tanh(half)

        for side in range(2):
            edge_act[side] = norm_silu(col_halo[phase, b, side])
        line = lax.broadcasted_iota(jnp.int32, (cols, chans), 0)

        def put(place, y, left, right):
            act[b, 1, place] = y.astype(BF16)
            before = jnp.where(line == 0, left, pltpu.roll(y, 1, axis=0))
            act[b, 0, place] = before.astype(BF16)
            after = jnp.where(line == cols - 1, right, pltpu.roll(y, cols - 1, axis=0))
            act[b, 2, place] = after.astype(BF16)

        @pl.loop(0, rows)
        def _(r):
            put(
                r + 1,
                norm_silu(field[b, r]),
                edge_act[0, pl.ds(r, 1), :],
                edge_act[1, pl.ds(r, 1), :],
            )

        for end, inside in ((0, lat > 0), (1, lat < n_lat - 1)):
            place = (rows + 1) * end

            @pl.when(inside)
            def _():
                put(
                    place,
                    norm_silu(row_halo[phase, b, end]),
                    norm_silu(corner_halo[phase, b, 2 * end]),
                    norm_silu(corner_halo[phase, b, 2 * end + 1]),
                )

            @pl.when(jnp.logical_not(inside))
            def _():
                for q in range(3):
                    act[b, q, place] = jnp.zeros((cols, chans), BF16)

    STEP = 8

    def convolve(k, b, finish):
        @pl.loop(0, rows // STEP)
        def _(chunk):
            base = chunk * STEP
            total = None
            for tap in range(9):
                p, q = divmod(tap, 3)
                window = act[b, q, pl.ds(base + p, STEP)].reshape(STEP * cols, chans)
                product = jnp.dot(window, weights[k, tap], preferred_element_type=F32)
                term = product.reshape(STEP, cols, chans) * scales[
                    k, pl.ds(base, STEP), tap : tap + 1, :
                ]
                total = term if total is None else total + term
            finish(base, total)

    def group_of(dim):
        index = lax.broadcasted_iota(jnp.int32, (chans, chans), dim).astype(F32)
        return jnp.floor((index + 0.5) * (1.0 / per_group))

    group_sum[...] = jnp.where(group_of(0) == group_of(1), 1.0, 0.0).astype(BF16)

    for k in range(2):

        @pl.loop(0, rows)
        def _(h):
            scales[k, h] = tap_scale[k, band[h]]

    for b in range(batch):

        def load_row(r, total, b=b):
            x = latent[b, r].astype(F32)
            field[b, r] = x
            return total + fold(x)

        total = lax.fori_loop(0, rows, load_row, jnp.zeros((8, chans), F32), unroll=4)
        if b == 0:
            pl.semaphore_wait(barrier, n - 1)
        start_halos(0, b)
        local_stats(0, b, total)
        start_stats(0, b)

    weight_copies[0].wait()
    for b in range(batch):
        average, slope = finish_stats(0, b)
        wait_halos(0, b)
        activate(0, b, average, slope)
        shift = time_shift[b : b + 1, :]

        def keep(base, total, b=b, shift=shift):
            field[b, pl.ds(base, STEP)] = total + shift[None]

        convolve(0, b, keep)
        start_halos(1, b)
        local_stats(1, b, local_sum(b))
        start_stats(1, b)

    weight_copies[1].wait()
    for b in range(batch):
        average, slope = finish_stats(1, b)
        wait_halos(1, b)
        activate(1, b, average, slope)

        def emit(base, total, b=b):
            place = pl.ds(base, STEP)
            out[b, place] = (latent[b, place].astype(F32) + total).astype(BF16)

        convolve(1, b, emit)

    for phase in range(2):
        for b in range(batch):
            stat_copy(phase, b, 1, n - 1).wait_send()


def solution(mesh):
    n_lon, n_lat = mesh.shape["lon"], mesh.shape["lat"]
    n = n_lon * n_lat

    def local(latent, band_index, time_shift, norm_gains, tap_scale, conv_one, conv_two):
        batch, rows, cols, chans = latent.shape
        taps = conv_one.shape[0]
        vmem = pl.BlockSpec(memory_space=pltpu.VMEM)
        smem = pl.BlockSpec(memory_space=pltpu.SMEM)
        anywhere = pl.BlockSpec(memory_space=pl.ANY)
        dma = pltpu.SemaphoreType.DMA
        return pl.pallas_call(
            functools.partial(kernel, n_lon, n_lat),
            out_shape=jax.ShapeDtypeStruct(latent.shape, latent.dtype),
            in_specs=[vmem, smem, vmem, vmem, vmem, anywhere, anywhere],
            out_specs=vmem,
            scratch_shapes=[
                pltpu.VMEM((batch, rows, cols, chans), F32),
                pltpu.VMEM((batch, 3, rows + 2, cols, chans), BF16),
                pltpu.VMEM((2, taps, chans, chans), BF16),
                pltpu.VMEM((2, rows, taps, chans), F32),
                pltpu.VMEM((2, batch, 2, cols, chans), F32),
                pltpu.VMEM((2, batch, 2, rows, chans), F32),
                pltpu.VMEM((2, batch, 4, 1, chans), F32),
                pltpu.VMEM((2, batch, 2, rows, chans), F32),
                pltpu.VMEM((2, batch, 4, 1, chans), F32),
                pltpu.VMEM((2, rows, chans), F32),
                pltpu.VMEM((2, batch, 2, chans), F32),
                pltpu.VMEM((2, batch, n, 2, chans), F32),
                pltpu.VMEM((chans, chans), BF16),
                dma((2,)),
                dma((2, batch, 8)),
                dma((2, batch, 8)),
                dma((2, batch)),
                dma((2, batch)),
            ],
            compiler_params=pltpu.CompilerParams(
                collective_id=0, has_side_effects=True, vmem_limit_bytes=48 * 1024 * 1024
            ),
            name="block",
        )(latent, band_index, time_shift, norm_gains, tap_scale, conv_one, conv_two)

    return jax.shard_map(
        local,
        mesh=mesh,
        in_specs=(P("groups", "lat", "lon", None), P("lat"), P("groups", None), P(), P(), P(), P()),
        out_specs=P("groups", "lat", "lon", None),
        check_vma=False,
    )
```

time: 189 us -> 41.7 us (0.22)
  blocking collectives: 124 us -> 0 us
  Pallas kernels: 0 us -> 34.5 us
  matrix products: 23.4 us -> 0 us
  starting transfers between devices: 13 us -> 0 us
  other arithmetic: 12 us -> 0 us
  local copies, waits for them, and re-layouts: 11.5 us -> 6.92 us
  waiting for transfers between devices: 2.03 us -> 0 us
    psum x4 -> x0, blocking collectives: 124 us -> none  [the longest x2 65.5 us: norm_silu(): summed = lax.psum(jnp.sum(grouped, axis=(1, 2, 4)), ('lon', 'lat'))]
    pallas_call x0 -> x1, Pallas kernels: none -> 34.5 us  [local(): pl.pallas_call(functools.partial(kernel, n_lon, n_lat), out_shape=jax.Sha...]
    dot_general x19 -> x0, matrix products: 23.4 us -> none  [the longest x18 23 us: convolve(): jnp.dot(window, kernel[tap_index], preferred_element_type=jnp.float32)]
    ppermute x8 -> x0, starting transfers between devices: 13 us -> none  [the longest x4 10.4 us: padded_2(): lax.ppermute(head, axis, [((i + 1) % count, i) for i in range(ends)])]
    reduce_sum x7 -> x0, other arithmetic: 5.36 us -> none  [the longest x4 2.84 us: norm_silu(): jnp.sum(jnp.square(centred), axis=(1, 2, 4))]
    concatenate x2 -> x0, other arithmetic: 4.32 us -> none  [padded_2(): jnp.concatenate([lax.ppermute(tail, axis, [(i, (i + 1) % count) for i in...]
    unnamed x43 -> x12, local copies, waits for them, and re-layouts: 3.32 us -> 6.92 us
    slice x6 -> x0, local copies, waits for them, and re-layouts: 2.75 us -> none  [the longest x2 1.04 us: convolve(): row_scales[None, :, None, tap_index, :]]
  transfers between devices with their start and end apart: 8 -> 0, of which waited for: 2 -> 0; matrix products, arithmetic and copies ran while one was open for 7% -> 0% of each run, Pallas kernels for 0% -> 0%
where the time goes in v1:
time: 41.7 us; the launch traced here: 41.4 us
  Pallas kernels  34.5 us (83%)
  local copies, waits for them, and re-layouts  6.92 us (17%)
    pallas_call x1, Pallas kernels, local(): pl.pallas_call(functools.partial(kernel, n_lon, n_lat), out_shape=jax.Sha...  34.5 us
    unnamed x12, local copies, waits for them, and re-layouts  6.92 us

profile of v1, /device:TPU:0, one launch (start us, length us, event | category | flops | bytes accessed | tf_op | source)
XLA Modules:
  0.0 41.4 jit_solution(10770099616701677473)
XLA Ops:
  0.0 1.0 %copy.8.tap_scale = f32[2,8,9,320]{3,2,1,0:T(8,128)S(1)} copy(f32[2,8,9,320]{3,1,2,0:T(8,128)} %param.11) | data formatting | bytes 368640 | tf_op args[4]
  1.0 0.0 copy-start
  1.0 1.6 %copy-done = bf16[9,320,320]{2,1,0:T(8,128)(2,1)S(1)} copy-done((bf16[9,320,320]{2,1,0:T(8,128)(2,1)S(1)}, bf16[9,320,320]{2,1,0:T(8,128)(2,1)}, u32[]{:S(2)}) %copy-start) | copy-done | bytes 1843224
  2.6 0.0 copy-start.1
  2.6 1.3 %copy-done.1 = bf16[2,24,32,320]{3,2,1,0:T(8,128)(2,1)S(1)} copy-done((bf16[2,24,32,320]{3,2,1,0:T(8,128)(2,1)S(1)}, bf16[2,24,32,320]{3,2,1,0:T(8,128)(2,1)}, u32[]{:S(2)}) %copy-start.1) | copy-done | bytes 983064
  3.9 0.0 copy-start.2
  3.9 0.7 %copy-done.2 = f32[2,320]{1,0:T(2,128)S(1)} copy-done((f32[2,320]{1,0:T(2,128)S(1)}, f32[2,320]{1,0:T(2,128)}, u32[]{:S(2)}) %copy-start.2) | copy-done | bytes 2584
  4.6 0.0 copy-start.3
  4.6 0.7 %copy-done.3 = f32[2,320]{1,0:T(2,128)S(1)} copy-done((f32[2,320]{1,0:T(2,128)S(1)}, f32[2,320]{1,0:T(2,128)}, u32[]{:S(2)}) %copy-start.3) | copy-done | bytes 2584
  5.3 0.0 copy-start.4
  5.3 0.7 %copy-done.4 = s32[24]{0:T(128)S(1)} copy-done((s32[24]{0:T(128)S(1)}, s32[24]{0:T(128)}, u32[]{:S(2)}) %copy-start.4) | copy-done | bytes 120
  5.9 34.5 %block.1 = bf16[2,24,32,320]{3,2,1,0:T(8,128)(2,1)S(1)} custom-call(bf16[2,24,32,320]{3,2,1,0:T(8,128)(2,1)S(1)} %copy-done.1, s32[24]{0:T(128)S(1)} %copy-done.4, f32[2,320]{1,0:T(2,128)S(1)} %copy-done.2, f32[2,320]{1,0:T(2,128)S(1)} %copy-done.3, f32[2,8,9,320]{3,2,1,0:T(8,128)S(1)} %copy.8.tap_scale, bf16[9,320,320]{2,1,0:T(8,128)(2,1)S(1)} %copy-done, ...), custom_call_target="tpu_custom_call" | custom-call | tf_op jit(solution)/shard_map/block/pallas_call | solution.py:320
  40.4 1.0 %copy.10 = bf16[2,24,32,320]{3,2,1,0:T(8,128)(2,1)} copy(bf16[2,24,32,320]{3,2,1,0:T(8,128)(2,1)S(1)} %block.1) | data formatting | bytes 1966080
Async XLA Ops:
  1.0 1.6 %copy-start = (bf16[9,320,320]{2,1,0:T(8,128)(2,1)S(1)}, bf16[9,320,320]{2,1,0:T(8,128)(2,1)}, u32[]{:S(2)}) copy-start(bf16[9,320,320]{2,1,0:T(8,128)(2,1)} %conv_one.1) | copy-start | bytes 5529604
  2.6 1.3 %copy-start.1 = (bf16[2,24,32,320]{3,2,1,0:T(8,128)(2,1)S(1)}, bf16[2,24,32,320]{3,2,1,0:T(8,128)(2,1)}, u32[]{:S(2)}) copy-start(bf16[2,24,32,320]{3,2,1,0:T(8,128)(2,1)} %latent.1) | copy-start | bytes 2949124
  3.9 0.7 %copy-start.2 = (f32[2,320]{1,0:T(2,128)S(1)}, f32[2,320]{1,0:T(2,128)}, u32[]{:S(2)}) copy-start(f32[2,320]{1,0:T(2,128)} %time_shift.1) | copy-start | bytes 7684
  4.6 0.7 %copy-start.3 = (f32[2,320]{1,0:T(2,128)S(1)}, f32[2,320]{1,0:T(2,128)}, u32[]{:S(2)}) copy-start(f32[2,320]{1,0:T(2,128)} %gains.1) | copy-start | bytes 7684
  5.3 0.7 %copy-start.4 = (s32[24]{0:T(128)S(1)}, s32[24]{0:T(128)}, u32[]{:S(2)}) copy-start(s32[24]{0:T(128)} %band.1) | copy-start | bytes 292

commit v2 on v1

--- a/solution.py
+++ b/solution.py
@@ -12,20 +12,30 @@
 MESH = pl.DeviceIdType.MESH
 F32 = jnp.float32
 BF16 = jnp.bfloat16
+WIDE = 256
+REST = 64
+STEP = 24
 WAYS = ((-1, 0), (1, 0), (0, -1), (0, 1), (-1, -1), (-1, 1), (1, -1), (1, 1))
 
 
 def kernel(
     n_lon,
     n_lat,
+    latent_hbm,
+    band_hbm,
+    time_shift_hbm,
+    gains_hbm,
+    tap_scale_hbm,
+    conv_one,
+    conv_two,
+    out,
     latent,
     band,
     time_shift,
     gains,
     tap_scale,
-    conv_one,
-    conv_two,
-    out,
+    table,
+    tails,
     field,
     act,
     weights,
@@ -39,6 +49,7 @@
     stat_send,
     stat_recv,
     group_sum,
+    load_sem,
     weight_sem,
     halo_send_sem,
     halo_recv_sem,
@@ -57,6 +68,21 @@
     def peer_id(step):
         peer = lax.rem(me + step, n)
         return {"lon": peer // n_lat, "lat": lax.rem(peer, n_lat)}
+
+    loads = [
+        pltpu.make_async_copy(src, dst, load_sem.at[i])
+        for i, (src, dst) in enumerate(
+            [(latent_hbm.at[b], latent.at[b]) for b in range(batch)]
+            + [
+                (tap_scale_hbm, tap_scale),
+                (band_hbm, band),
+                (gains_hbm, gains),
+                (time_shift_hbm, time_shift),
+            ]
+        )
+    ]
+    for copy in loads:
+        copy.start()
 
     barrier = pltpu.get_barrier_semaphore()
 
@@ -108,7 +134,7 @@
     def start_halos(phase, b):
         for side, col in ((0, 0), (1, cols - 1)):
 
-            @pl.loop(0, rows)
+            @pl.loop(0, rows, unroll=8)
             def _(r):
                 col_send[phase, b, side, pl.ds(r, 1), :] = field[b, r, col : col + 1, :]
 
@@ -116,6 +142,8 @@
             ((0, 0), (0, cols - 1), (rows - 1, 0), (rows - 1, cols - 1))
         ):
             corner_send[phase, b, mine] = field[b, r, c : c + 1, :]
+        if phase == 0 and b == 0:
+            pl.semaphore_wait(barrier, n - 1)
         for way, (d_lat, _) in enumerate(WAYS):
             when_lat(d_lat, lambda way=way: halo_copy(phase, b, way).start())
 
@@ -205,7 +233,7 @@
             after = jnp.where(line == cols - 1, right, pltpu.roll(y, cols - 1, axis=0))
             act[b, 2, place] = after.astype(BF16)
 
-        @pl.loop(0, rows)
+        @pl.loop(0, rows, unroll=2)
         def _(r):
             put(
                 r + 1,
@@ -231,22 +259,37 @@
                 for q in range(3):
                     act[b, q, place] = jnp.zeros((cols, chans), BF16)
 
-    STEP = 8
-
     def convolve(k, b, finish):
         @pl.loop(0, rows // STEP)
         def _(chunk):
             base = chunk * STEP
-            total = None
-            for tap in range(9):
-                p, q = divmod(tap, 3)
-                window = act[b, q, pl.ds(base + p, STEP)].reshape(STEP * cols, chans)
-                product = jnp.dot(window, weights[k, tap], preferred_element_type=F32)
-                term = product.reshape(STEP, cols, chans) * scales[
-                    k, pl.ds(base, STEP), tap : tap + 1, :
-                ]
-                total = term if total is None else total + term
-            finish(base, total)
+
+            def scale(tap, low, high):
+                return scales[k, pl.ds(base, STEP), tap : tap + 1, low:high]
+
+            body = even = odd = None
+            for q in range(3):
+                for p in range(3):
+                    window = act[b, q, pl.ds(base + p, STEP)].reshape(STEP * cols, chans)
+                    product = jnp.dot(
+                        window, weights[k, 3 * p + q, :, :WIDE], preferred_element_type=F32
+                    )
+                    term = product.reshape(STEP, cols, WIDE) * scale(3 * p + q, 0, WIDE)
+                    body = term if body is None else body + term
+                window = act[b, q, pl.ds(base, STEP + 2)].reshape((STEP + 2) * cols, chans)
+                product = jnp.dot(window, tails[k, q], preferred_element_type=F32)
+                product = product.reshape(STEP + 2, cols, 4 * REST)
+                side = [scale(3 * p + q, WIDE, WIDE + 2 * REST) for p in range(3)]
+                ends = (
+                    product[:STEP, :, : 2 * REST] * side[0]
+                    + product[2:, :, 2 * REST :] * side[2]
+                )
+                mid = product[1 : STEP + 1, :, : 2 * REST] * side[1]
+                even = ends if even is None else even + ends
+                odd = mid if odd is None else odd + mid
+            odd = pltpu.roll(odd.reshape(STEP * cols, 2 * REST), REST, axis=1)
+            rest = (even + odd.reshape(STEP, cols, 2 * REST))[:, :, :REST]
+            finish(base, jnp.concatenate([body, rest], axis=-1))
 
     def group_of(dim):
         index = lax.broadcasted_iota(jnp.int32, (chans, chans), dim).astype(F32)
@@ -254,13 +297,8 @@
 
     group_sum[...] = jnp.where(group_of(0) == group_of(1), 1.0, 0.0).astype(BF16)
 
-    for k in range(2):
-
-        @pl.loop(0, rows)
-        def _(h):
-            scales[k, h] = tap_scale[k, band[h]]
-
     for b in range(batch):
+        loads[b].wait()
 
         def load_row(r, total, b=b):
             x = latent[b, r].astype(F32)
@@ -268,13 +306,28 @@
             return total + fold(x)
 
         total = lax.fori_loop(0, rows, load_row, jnp.zeros((8, chans), F32), unroll=4)
-        if b == 0:
-            pl.semaphore_wait(barrier, n - 1)
         start_halos(0, b)
         local_stats(0, b, total)
         start_stats(0, b)
 
-    weight_copies[0].wait()
+    for copy in loads[batch:]:
+        copy.wait()
+    for k in range(2):
+        for tap in range(9):
+            lines = tap_scale[k, tap]
+            lines = jnp.concatenate([lines, lines[:, WIDE:]], axis=1)
+            for line in range(lines.shape[0]):
+                table[k, line, tap : tap + 1] = lines[line : line + 1]
+
+        @pl.loop(0, rows, unroll=4)
+        def _(h):
+            scales[k, h] = table[k, band[h]]
+
+        weight_copies[k].wait()
+        for q in range(3):
+            parts = [weights[k, 3 * p + q, :, WIDE:] for p in range(3)]
+            tails[k, q] = jnp.concatenate(parts + [jnp.zeros((chans, REST), BF16)], axis=1)
+
     for b in range(batch):
         average, slope = finish_stats(0, b)
         wait_halos(0, b)
@@ -289,7 +342,6 @@
         local_stats(1, b, local_sum(b))
         start_stats(1, b)
 
-    weight_copies[1].wait()
     for b in range(batch):
         average, slope = finish_stats(1, b)
         wait_halos(1, b)
@@ -314,19 +366,27 @@
         batch, rows, cols, chans = latent.shape
         taps = conv_one.shape[0]
         vmem = pl.BlockSpec(memory_space=pltpu.VMEM)
-        smem = pl.BlockSpec(memory_space=pltpu.SMEM)
-        anywhere = pl.BlockSpec(memory_space=pl.ANY)
+        hbm = pl.BlockSpec(memory_space=pltpu.HBM)
+        bands = tap_scale.shape[1]
         dma = pltpu.SemaphoreType.DMA
+        by_tap = jnp.transpose(tap_scale, (0, 2, 1, 3))
         return pl.pallas_call(
             functools.partial(kernel, n_lon, n_lat),
             out_shape=jax.ShapeDtypeStruct(latent.shape, latent.dtype),
-            in_specs=[vmem, smem, vmem, vmem, vmem, anywhere, anywhere],
+            in_specs=[hbm] * 7,
             out_specs=vmem,
             scratch_shapes=[
+                pltpu.VMEM(latent.shape, BF16),
+                pltpu.SMEM(band_index.shape, jnp.int32),
+                pltpu.VMEM(time_shift.shape, F32),
+                pltpu.VMEM(norm_gains.shape, F32),
+                pltpu.VMEM((2, taps, bands, chans), F32),
+                pltpu.VMEM((2, bands, taps, WIDE + 2 * REST), F32),
+                pltpu.VMEM((2, 3, chans, 4 * REST), BF16),
                 pltpu.VMEM((batch, rows, cols, chans), F32),
                 pltpu.VMEM((batch, 3, rows + 2, cols, chans), BF16),
                 pltpu.VMEM((2, taps, chans, chans), BF16),
-                pltpu.VMEM((2, rows, taps, chans), F32),
+                pltpu.VMEM((2, rows, taps, WIDE + 2 * REST), F32),
                 pltpu.VMEM((2, batch, 2, cols, chans), F32),
                 pltpu.VMEM((2, batch, 2, rows, chans), F32),
                 pltpu.VMEM((2, batch, 4, 1, chans), F32),
@@ -336,6 +396,7 @@
                 pltpu.VMEM((2, batch, 2, chans), F32),
                 pltpu.VMEM((2, batch, n, 2, chans), F32),
                 pltpu.VMEM((chans, chans), BF16),
+                dma((batch + 4,)),
                 dma((2,)),
                 dma((2, batch, 8)),
                 dma((2, batch, 8)),
@@ -343,10 +404,10 @@
                 dma((2, batch)),
             ],
             compiler_params=pltpu.CompilerParams(
-                collective_id=0, has_side_effects=True, vmem_limit_bytes=48 * 1024 * 1024
+                collective_id=0, has_side_effects=True, vmem_limit_bytes=int(62 * 1024 * 1024)
             ),
             name="block",
-        )(latent, band_index, time_shift, norm_gains, tap_scale, conv_one, conv_two)
+        )(latent, band_index, time_shift, norm_gains, by_tap, conv_one, conv_two)
 
     return jax.shard_map(
         local,

time: 41.7 us -> 34 us (0.82)
  local copies, waits for them, and re-layouts: 6.92 us -> 2.41 us
  Pallas kernels: 34.5 us -> 31.4 us
    unnamed x12 -> x1, local copies, waits for them, and re-layouts: 6.92 us -> 2.41 us
    pallas_call x1, Pallas kernels: 34.5 us -> 31.4 us  [local(): pl.pallas_call(functools.partial(kernel, n_lon, n_lat), out_shape=jax.Sha...]
where the time goes in v2:
time: 34 us; the launch traced here: 33.8 us
  Pallas kernels  31.4 us (92%)
  local copies, waits for them, and re-layouts  2.41 us (7%)
    pallas_call x1, Pallas kernels, local(): pl.pallas_call(functools.partial(kernel, n_lon, n_lat), out_shape=jax.Sha...  31.4 us
    unnamed x1, local copies, waits for them, and re-layouts  2.41 us

profile of v2, /device:TPU:0, one launch (start us, length us, event | category | flops | bytes accessed | tf_op | source)
XLA Modules:
  0.0 33.8 jit_solution(15660322718578805593)
XLA Ops:
  0.0 31.4 %block.1 = bf16[2,24,32,320]{3,2,1,0:T(8,128)(2,1)} custom-call(bf16[2,24,32,320]{3,2,1,0:T(8,128)(2,1)} %latent_hbm.1, s32[24]{0:T(128)} %band_hbm.1, f32[2,320]{1,0:T(2,128)} %time_shift_hbm.1, f32[2,320]{1,0:T(2,128)} %gains_hbm.1, f32[2,9,8,320]{3,2,1,0:T(8,128)} %bitcast.1, bf16[9,320,320]{2,1,0:T(8,128)(2,1)} %conv_one.1, bf16[9,320,320]{2,1,0:T(8,128)(2,1)} %conv_two.1), custom_call_target="tpu_custom_call" | custom-call | tf_op jit(solution)/shard_map/block/pallas_call | solution.py:373
  31.4 2.4 %copy.9 = bf16[2,24,32,320]{3,2,1,0:T(8,128)(2,1)} copy(bf16[2,24,32,320]{3,2,1,0:T(8,128)(2,1)} %block.1) | data formatting | bytes 1966080

commit v3 on v2

--- a/solution.py
+++ b/solution.py
@@ -50,6 +50,7 @@
     stat_recv,
     group_sum,
     load_sem,
+    store_sem,
     weight_sem,
     halo_send_sem,
     halo_recv_sem,
@@ -90,6 +91,9 @@
     def _(step):
         pl.semaphore_signal(barrier, inc=1, device_id=peer_id(step), device_id_type=MESH)
 
+    stores = [
+        pltpu.make_async_copy(latent.at[b], out.at[b], store_sem.at[b]) for b in range(batch)
+    ]
     weight_copies = [
         pltpu.make_async_copy(src, weights.at[k], weight_sem.at[k])
         for k, src in enumerate((conv_one, conv_two))
@@ -173,7 +177,7 @@
         def body(r, total):
             return total + fold(field[b, r])
 
-        return lax.fori_loop(0, rows, body, jnp.zeros((8, chans), F32), unroll=4)
+        return lax.fori_loop(0, rows, body, jnp.zeros((8, chans), F32), unroll=8)
 
     def stat_copy(phase, b, step, span):
         return pltpu.make_async_remote_copy(
@@ -195,7 +199,7 @@
             centred = field[b, r] - average
             return squares + fold(centred * centred)
 
-        squares = lax.fori_loop(0, rows, body, jnp.zeros((8, chans), F32), unroll=4)
+        squares = lax.fori_loop(0, rows, body, jnp.zeros((8, chans), F32), unroll=8)
         squares = jnp.sum(squares, axis=0, keepdims=True)
         stat_send[phase, b, 0:1] = summed
         stat_send[phase, b, 1:2] = squares
@@ -233,7 +237,7 @@
             after = jnp.where(line == cols - 1, right, pltpu.roll(y, cols - 1, axis=0))
             act[b, 2, place] = after.astype(BF16)
 
-        @pl.loop(0, rows, unroll=2)
+        @pl.loop(0, rows, unroll=6)
         def _(r):
             put(
                 r + 1,
@@ -305,7 +309,7 @@
             field[b, r] = x
             return total + fold(x)
 
-        total = lax.fori_loop(0, rows, load_row, jnp.zeros((8, chans), F32), unroll=4)
+        total = lax.fori_loop(0, rows, load_row, jnp.zeros((8, chans), F32), unroll=8)
         start_halos(0, b)
         local_stats(0, b, total)
         start_stats(0, b)
@@ -319,7 +323,7 @@
             for line in range(lines.shape[0]):
                 table[k, line, tap : tap + 1] = lines[line : line + 1]
 
-        @pl.loop(0, rows, unroll=4)
+        @pl.loop(0, rows, unroll=8)
         def _(h):
             scales[k, h] = table[k, band[h]]
 
@@ -349,13 +353,16 @@
 
         def emit(base, total, b=b):
             place = pl.ds(base, STEP)
-            out[b, place] = (latent[b, place].astype(F32) + total).astype(BF16)
+            latent[b, place] = (latent[b, place].astype(F32) + total).astype(BF16)
 
         convolve(1, b, emit)
+        stores[b].start()
 
     for phase in range(2):
         for b in range(batch):
             stat_copy(phase, b, 1, n - 1).wait_send()
+    for copy in stores:
+        copy.wait()
 
 
 def solution(mesh):
@@ -365,7 +372,6 @@
     def local(latent, band_index, time_shift, norm_gains, tap_scale, conv_one, conv_two):
         batch, rows, cols, chans = latent.shape
         taps = conv_one.shape[0]
-        vmem = pl.BlockSpec(memory_space=pltpu.VMEM)
         hbm = pl.BlockSpec(memory_space=pltpu.HBM)
         bands = tap_scale.shape[1]
         dma = pltpu.SemaphoreType.DMA
@@ -374,7 +380,7 @@
             functools.partial(kernel, n_lon, n_lat),
             out_shape=jax.ShapeDtypeStruct(latent.shape, latent.dtype),
             in_specs=[hbm] * 7,
-            out_specs=vmem,
+            out_specs=hbm,
             scratch_shapes=[
                 pltpu.VMEM(latent.shape, BF16),
                 pltpu.SMEM(band_index.shape, jnp.int32),
@@ -397,6 +403,7 @@
                 pltpu.VMEM((2, batch, n, 2, chans), F32),
                 pltpu.VMEM((chans, chans), BF16),
                 dma((batch + 4,)),
+                dma((batch,)),
                 dma((2,)),
                 dma((2, batch, 8)),
                 dma((2, batch, 8)),

time: 34 us -> 33.5 us (0.985)
  Pallas kernels: 31.4 us -> 31 us
    pallas_call x1, Pallas kernels: 31.4 us -> 31 us  [local(): pl.pallas_call(functools.partial(kernel, n_lon, n_lat), out_shape=jax.Sha...]
where the time goes in v3:
time: 33.5 us; the launch traced here: 33.4 us
  Pallas kernels  31 us (93%)
  local copies, waits for them, and re-layouts  2.41 us (7%)
    pallas_call x1, Pallas kernels, local(): pl.pallas_call(functools.partial(kernel, n_lon, n_lat), out_shape=jax.Sha...  31 us
    unnamed x1, local copies, waits for them, and re-layouts  2.41 us

profile of v3, /device:TPU:0, one launch (start us, length us, event | category | flops | bytes accessed | tf_op | source)
XLA Modules:
  0.0 33.4 jit_solution(9392451239035717742)
XLA Ops:
  0.0 31.0 %block.1 = bf16[2,24,32,320]{3,2,1,0:T(8,128)(2,1)} custom-call(bf16[2,24,32,320]{3,2,1,0:T(8,128)(2,1)} %latent_hbm.1, s32[24]{0:T(128)} %band_hbm.1, f32[2,320]{1,0:T(2,128)} %time_shift_hbm.1, f32[2,320]{1,0:T(2,128)} %gains_hbm.1, f32[2,9,8,320]{3,2,1,0:T(8,128)} %bitcast.1, bf16[9,320,320]{2,1,0:T(8,128)(2,1)} %conv_one.1, bf16[9,320,320]{2,1,0:T(8,128)(2,1)} %conv_two.1), custom_call_target="tpu_custom_call" | custom-call | tf_op jit(solution)/shard_map/block/pallas_call | solution.py:379
  31.0 2.4 %copy.9 = bf16[2,24,32,320]{3,2,1,0:T(8,128)(2,1)} copy(bf16[2,24,32,320]{3,2,1,0:T(8,128)(2,1)} %block.1) | data formatting | bytes 1966080
